TPU v7x, 32 devices: a whole 2x2x4 slice. The times are simulated.
32 devices in a mesh: row: 8 (over z, core), col: 4 (over y, x).
Axes of the slice: x: 2, y: 2, z: 4, core: 2. Of those that a mesh axis runs over, the one named last changes fastest.
Arguments:
- spans: bfloat16 [4096, 768], P(('row', 'col')), may hold values from -10 to 10
- centroids: bfloat16 [2048, 768], P(('col', 'row')), may hold values from -10 to 10
- pattern: int32 [32, 4], P('row'), may hold values from 0 to 15, as said below
Outputs:
- new_centroids: bfloat16 [2048, 768], P(('col', 'row'))
- row_potential: float32 [4096], P('row')
- col_potential: float32 [2048], P('col')
Inputs may be any that keep to these rules, and one draw needn't show every extreme that they name: `pattern`: each row lists 4 distinct centroid blocks in rising order; row b always lists block b % 16; every centroid block is listed by some row.
All inputs are finite; a program needn't handle non-finite values.
Results may differ from a plain program's by a relative error of at most 0.0095.
Values may be sent and summed in bfloat16 or wider, within the bound.
No kernel may reach another device: no remote copies, remote signals or barrier semaphores. Data moves between devices by JAX's collectives and lax.ppermute only.
A program may use at most 64 MiB of HBM per device.

v0:
```python
import math

import jax
import jax.numpy as jnp
from jax import lax
from jax.sharding import PartitionSpec as P

ITERS = 3


logit_scale = 0.0625
floor_value = -1e30


def swap(x, axis, k, one_core=False):
    if not one_core:
        return lax.ppermute(x, axis, [(i, i ^ k) for i in range(lax.axis_size(axis))])
    cols = lax.axis_size("col")
    k = k * cols if axis == "row" else k
    pairs = [(i, i ^ k if i // cols & 1 else i) for i in range(lax.axis_size("row") * cols)]
    return lax.ppermute(x, ("row", "col"), pairs)


def stages(axis):
    low = 1 if axis == "row" else 0
    bits = (lax.axis_size(axis) - 1).bit_length()
    return [(at, 1 << min(2, bits - at)) for at in range(low, bits, 2)]


def digit(axis, at, size):
    return (lax.axis_index(axis) >> at) & (size - 1)


def place(parts, index):
    whole = jnp.zeros((len(parts),) + parts[0].shape, parts[0].dtype)
    for d, part in enumerate(parts):
        whole = lax.dynamic_update_index_in_dim(whole, part, index ^ d, 0)
    return whole.reshape((-1,) + parts[0].shape[1:])


def gather_blocks(x, axis):
    for at, size in stages(axis):
        parts = [x] + [swap(x, axis, d << at) for d in range(1, size)]
        x = place(parts, digit(axis, at, size))
    return x


def both_cores(x):
    return place([x, swap(x, "row", 1)], lax.axis_index("row") % 2)


def tree(op, parts):
    while len(parts) > 1:
        parts = [op(parts[i], parts[i + 1]) for i in range(0, len(parts), 2)]
    return parts[0]


def log_sum_over(x, axis):
    terms = []
    for at, size in stages(axis):
        parts = [x] + [swap(x, axis, d << at, one_core=True) for d in range(1, size)]
        high = tree(jnp.maximum, parts)
        x = high + jnp.log(tree(jnp.add, [jnp.exp(part - high) for part in parts]))
        terms.append(parts)
    return x, terms


def per_device(spans, centroids, pattern):
    rows, cols = lax.axis_size("row"), lax.axis_size("col")
    chips = rows // 2
    me_row, me_col = lax.axis_index("row"), lax.axis_index("col")
    core = me_row % 2
    per = centroids.shape[0]
    half_cols = per * chips
    group_cols = 2 * half_cols
    row_count = spans.shape[0] * cols

    chip_lists = both_cores(pattern)
    tile_centroids = both_cores(gather_blocks(centroids, "row"))
    tile_spans = both_cores(gather_blocks(spans, "col"))
    row_blocks = jnp.repeat(chip_lists, 128, axis=0)
    place_in_group = jnp.arange(group_cols)
    row_of = place_in_group % half_cols // per * 2 + place_in_group // half_cols
    col_block = (me_col * group_cols + row_of * per + place_in_group % per) // 128
    allowed_cells = jnp.any(row_blocks[:, :, None] == col_block[None, None, :], axis=1)
    scores = (
        lax.dot_general(
            tile_spans, tile_centroids, (((1,), (1,)), ((), ())), preferred_element_type=jnp.float32
        )
        * logit_scale
    )
    scores = jnp.where(allowed_cells, scores, floor_value)
    mass_ratio = group_cols * cols / (row_count * rows)
    log_target = -math.log(mass_ratio)
    col_pot = jnp.zeros((group_cols,), jnp.float32)
    for sweep in range(ITERS):
        shifted = scores + col_pot[None, :]
        row_high = jnp.max(shifted, axis=1)
        row_sum = jnp.sum(jnp.exp(shifted - row_high[:, None]), axis=1)
        row_log, unused = log_sum_over(row_high + jnp.log(row_sum), "col")
        row_pot = -row_log
        if sweep == ITERS - 1:
            row_pot = jnp.where(core == 1, row_pot, swap(row_pot, "row", 1))
        shifted = scores + row_pot[:, None]
        col_high = jnp.max(shifted, axis=0)
        weights = jnp.exp(shifted - col_high[None, :])
        col_sum = jnp.sum(weights, axis=0)
        col_log, terms = log_sum_over(col_high + jnp.log(col_sum), "row")
        col_pot = log_target - col_log

    own_weights = lax.dynamic_slice_in_dim(weights, core * half_cols, half_cols, 1)
    own_sum = lax.dynamic_slice_in_dim(col_sum, core * half_cols, half_cols, 0)
    averages = (
        lax.dot_general(
            own_weights.astype(jnp.bfloat16),
            tile_spans,
            (((0,), (0,)), ((), ())),
            preferred_element_type=jnp.float32,
        )
        / own_sum[:, None]
    )
    flat = [part for parts in terms for part in parts]
    got = swap(jnp.concatenate([col_pot] + [part[:half_cols] for part in flat]), "row", 1)
    mine = jnp.concatenate([col_pot] + [part[half_cols:] for part in flat])
    both = jnp.where(core == 1, mine, got)
    col_pot = both[:group_cols]
    logs = both[group_cols:].reshape(-1, half_cols)

    held = averages.reshape((chips, per) + averages.shape[1:])
    first = 0
    for number, (at, size) in enumerate(stages("row")):
        me = digit("row", at, size)
        held = held.reshape((-1, size) + held.shape[1:])
        own = lax.dynamic_index_in_dim(held, me, 1, keepdims=False)
        low = held.astype(jnp.bfloat16)
        parts = [own] + [
            swap(lax.dynamic_index_in_dim(low, me ^ d, 1, keepdims=False), "row", d << at).astype(jnp.float32)
            for d in range(1, size)
        ]
        share = logs[first : first + size].reshape(size, chips, per)
        for done_at, done_size in stages("row")[: number + 1]:
            share = share.reshape(size, -1, done_size, per)
            share = lax.dynamic_index_in_dim(share, digit("row", done_at, done_size), 2, keepdims=False)
        share = jnp.exp(share - jnp.max(share, axis=0))
        share = share / jnp.sum(share, axis=0)
        held = tree(jnp.add, [share[d][:, :, None] * parts[d] for d in range(size)])
        first += size
    centroid_sum = held.reshape(per, -1) * math.exp(log_target)
    return (
        (centroid_sum * mass_ratio).astype(jnp.bfloat16),
        lax.dynamic_slice_in_dim(row_pot, core * row_count, row_count, 0),
        col_pot.reshape(2, chips, per).swapaxes(0, 1).reshape(-1),
    )


def solution(mesh):
    placed = (P(("row", "col"), None), P(("col", "row"), None), P("row", None))
    return jax.shard_map(
        per_device,
        mesh=mesh,
        in_specs=placed,
        out_specs=(P(("col", "row"), None), P("row"), P("col")),
        check_vma=False,
    )
```

profile of v0, /device:TPU:0, one launch (start us, length us, event | category | flops | bytes accessed | tf_op | source)
XLA Modules:
  0.0 111.0 jit_solution(3279352107066703630)
XLA Ops:
  0.6 3.0 %collective-permute-start.1 = (bf16[128,768]{1,0:T(8,128)(2,1)}, bf16[128,768]{1,0:T(8,128)(2,1)S(1)}, u32[]{:S(2)}, u32[]{:S(2)}) collective-permute-start(bf16[128,768]{1,0:T(8,128)(2,1)} %param.3), channel_id=1, source_target_pairs={{0,1},{1,0},{2,3},{3,2},{4,5},{5,4},{6,7},{7,6},{8,9},{9,8},{10,11... | collective-permute-start | bytes 589832 | tf_op jit(solution)/shard_map/ppermute | solution.py:17
  3.6 1.5 %collective-permute-start.2 = (bf16[128,768]{1,0:T(8,128)(2,1)}, bf16[128,768]{1,0:T(8,128)(2,1)S(1)}, u32[]{:S(2)}, u32[]{:S(2)}) collective-permute-start(bf16[128,768]{1,0:T(8,128)(2,1)} %param.3), channel_id=1, source_target_pairs={{0,2},{1,3},{2,0},{3,1},{4,6},{5,7},{6,4},{7,5},{8,10},{9,11},{10,... | collective-permute-start | bytes 589832 | tf_op jit(solution)/shard_map/ppermute | solution.py:17
  5.2 2.0 %collective-permute-start.5 = (bf16[64,768]{1,0:T(8,128)(2,1)}, bf16[64,768]{1,0:T(8,128)(2,1)S(1)}, u32[]{:S(2)}, u32[]{:S(2)}) collective-permute-start(bf16[64,768]{1,0:T(8,128)(2,1)} %param.4), channel_id=1, source_target_pairs={{0,8},{4,12},{8,0},{12,4},{16,24},{20,28},{24,16},{28,20},{1,9},{5... | collective-permute-start | bytes 294920 | tf_op jit(solution)/shard_map/ppermute | solution.py:17
  7.2 0.8 copy.16
  8.1 0.9 bitcast_dynamic-update-slice_fusion.7
  9.1 0.9 bitcast_dynamic-update-slice_fusion.11
  10.0 2.7 %collective-permute-start.6 = (bf16[64,768]{1,0:T(8,128)(2,1)}, bf16[64,768]{1,0:T(8,128)(2,1)S(1)}, u32[]{:S(2)}, u32[]{:S(2)}) collective-permute-start(bf16[64,768]{1,0:T(8,128)(2,1)} %param.4), channel_id=1, source_target_pairs={{0,16},{4,20},{8,24},{12,28},{16,0},{20,4},{24,8},{28,12},{1,17},{... | collective-permute-start | bytes 294920 | tf_op jit(solution)/shard_map/ppermute | solution.py:17
  13.0 1.1 collective-permute-start.7
  14.1 6.4 %collective-permute-done.6 = bf16[64,768]{1,0:T(8,128)(2,1)S(1)} collective-permute-done((bf16[64,768]{1,0:T(8,128)(2,1)}, bf16[64,768]{1,0:T(8,128)(2,1)S(1)}, u32[]{:S(2)}, u32[]{:S(2)}) %collective-permute-start.6) | collective-permute-done | bytes 98336 | tf_op jit(solution)/shard_map/ppermute | solution.py:17
  21.3 1.3 %compare_reduce_fusion = pred[1024,512]{1,0:T(8,128)(4,1)S(1)} fusion(s32[512]{0:T(512)S(1)} %add_select_fusion, s32[1024,4]{0,1:T(4,128)S(1)} %bitcast.86), kind=kLoop, calls=%fused_computation | loop fusion | flops 3670016 | bytes 542720 | tf_op jit(solution)/shard_map/reduce_or | solution.py:85
  22.9 0.7 collective-permute-done.8
  23.7 1.1 %fusion.47 = (f32[1024]{0:T(1024)S(1)}, f32[1024,512]{1,0:T(8,128)S(1)}) fusion(pred[1024,512]{1,0:T(8,128)(4,1)S(1)} %compare_reduce_fusion, bf16[1024,768]{1,0:T(8,128)(2,1)S(1)} %bitcast.79, bf16[512,768]{1,0:T(8,128)(2,1)S(1)} %bitcast.85), kind=kOutput, calls=%fused_computation.138 | convolution fusion | flops 806878208 | bytes 4984832 | tf_op jit(solution)/shard_map/dot_general | solution.py:87
  24.8 0.7 exponential_reduce_fusion.4
  25.5 0.7 collective-permute-start.10
  26.2 0.7 collective-permute-start.11
  26.9 0.7 collective-permute-start.9
  28.3 0.7 collective-permute-start.12
  29.0 0.7 collective-permute-start.13
  29.6 0.7 collective-permute-start.14
  31.2 0.7 collective-permute-start.15
  31.8 0.7 collective-permute-start.16
  33.9 0.7 collective-permute-start.18
  34.6 0.7 collective-permute-start.19
  35.2 0.7 collective-permute-start.20
  38.8 45.6 %collective-permute-start.24 = (f32[1024]{0:T(1024)S(1)}, f32[1024]{0:T(1024)S(1)}, u32[]{:S(2)}, u32[]{:S(2)}) collective-permute-start(f32[1024]{0:T(1024)S(1)} %add_negate_fusion), channel_id=1, source_target_pairs={{0,4},{4,0},{8,12},{12,8},{16,20},{20,16},{24,28},{28,24},{1,5},{5... | collective-permute-start | bytes 12296 | tf_op jit(solution)/shard_map/ppermute | solution.py:17
  84.4 0.8 collective-permute-done.24
  88.8 10.4 %collective-permute-start.28 = (f32[1536]{0:T(1024)S(1)}, f32[1536]{0:T(1024)S(1)}, u32[]{:S(2)}, u32[]{:S(2)}) collective-permute-start(f32[1536]{0:T(1024)S(1)} %get-tuple-element.16), channel_id=1, source_target_pairs={{0,4},{4,0},{8,12},{12,8},{16,20},{20,16},{24,28},{28,24},{1,5},{5... | collective-permute-start | bytes 18440 | tf_op jit(solution)/shard_map/ppermute | solution.py:17
  99.3 1.6 %collective-permute-start.30 = (bf16[1,64,768]{2,1,0:T(8,128)(2,1)S(1)}, bf16[1,64,768]{2,1,0:T(8,128)(2,1)S(1)}, u32[]{:S(2)}, u32[]{:S(2)}) collective-permute-start(bf16[1,64,768]{2,1,0:T(8,128)(2,1)S(1)} %get-tuple-element.11), channel_id=1, source_target_pairs={{0,16},{4,20},{8,24},{12,28},{16,0},{20,4},{24,8},{28,12},{1,17},{... | collective-permute-start | bytes 294920 | tf_op jit(solution)/shard_map/ppermute | solution.py:17
  100.9 2.8 %collective-permute-start.31 = (bf16[1,64,768]{2,1,0:T(8,128)(2,1)S(1)}, bf16[1,64,768]{2,1,0:T(8,128)(2,1)S(1)}, u32[]{:S(2)}, u32[]{:S(2)}) collective-permute-start(bf16[1,64,768]{2,1,0:T(8,128)(2,1)S(1)} %get-tuple-element.10), channel_id=1, source_target_pairs={{0,24},{4,28},{8,16},{12,20},{16,8},{20,12},{24,0},{28,4},{1,25},{... | collective-permute-start | bytes 294920 | tf_op jit(solution)/shard_map/ppermute | solution.py:17
  104.6 0.7 reshape.273
  105.3 4.9 %collective-permute-done.30 = bf16[1,64,768]{2,1,0:T(8,128)(2,1)S(1)} collective-permute-done((bf16[1,64,768]{2,1,0:T(8,128)(2,1)S(1)}, bf16[1,64,768]{2,1,0:T(8,128)(2,1)S(1)}, u32[]{:S(2)}, u32[]{:S(2)}) %collective-permute-start.30) | collective-permute-done | bytes 98336 | tf_op jit(solution)/shard_map/ppermute | solution.py:17
  110.2 0.8 fusion.3
  (111 shorter events, 11.7 us)
Async XLA Ops:
  0.6 19.9 %collective-permute-start.1 = (bf16[128,768]{1,0:T(8,128)(2,1)}, bf16[128,768]{1,0:T(8,128)(2,1)S(1)}, u32[]{:S(2)}, u32[]{:S(2)}) collective-permute-start(bf16[128,768]{1,0:T(8,128)(2,1)} %param.3), channel_id=1, source_target_pairs={{0,1},{1,0},{2,3},{3,2},{4,5},{5,4},{6,7},{7,6},{8,9},{9,8},{10,11... | collective-permute-start | bytes 589832 | tf_op jit(solution)/shard_map/ppermute | solution.py:17
  3.6 16.9 %collective-permute-start.2 = (bf16[128,768]{1,0:T(8,128)(2,1)}, bf16[128,768]{1,0:T(8,128)(2,1)S(1)}, u32[]{:S(2)}, u32[]{:S(2)}) collective-permute-start(bf16[128,768]{1,0:T(8,128)(2,1)} %param.3), channel_id=1, source_target_pairs={{0,2},{1,3},{2,0},{3,1},{4,6},{5,7},{6,4},{7,5},{8,10},{9,11},{10,... | collective-permute-start | bytes 589832 | tf_op jit(solution)/shard_map/ppermute | solution.py:17
  5.2 15.5 %collective-permute-start.3 = (bf16[128,768]{1,0:T(8,128)(2,1)}, bf16[128,768]{1,0:T(8,128)(2,1)S(1)}, u32[]{:S(2)}, u32[]{:S(2)}) collective-permute-start(bf16[128,768]{1,0:T(8,128)(2,1)} %param.3), channel_id=1, source_target_pairs={{0,3},{1,2},{2,1},{3,0},{4,7},{5,6},{6,5},{7,4},{8,11},{9,10},{10,... | collective-permute-start | bytes 589832 | tf_op jit(solution)/shard_map/ppermute | solution.py:17
  5.2 7.8 %collective-permute-start.5 = (bf16[64,768]{1,0:T(8,128)(2,1)}, bf16[64,768]{1,0:T(8,128)(2,1)S(1)}, u32[]{:S(2)}, u32[]{:S(2)}) collective-permute-start(bf16[64,768]{1,0:T(8,128)(2,1)} %param.4), channel_id=1, source_target_pairs={{0,8},{4,12},{8,0},{12,4},{16,24},{20,28},{24,16},{28,20},{1,9},{5... | collective-permute-start | bytes 294920 | tf_op jit(solution)/shard_map/ppermute | solution.py:17
  7.2 2.8 %collective-permute-start = (s32[4,4]{1,0:T(4,128)}, s32[4,4]{1,0:T(4,128)S(1)}, u32[]{:S(2)}, u32[]{:S(2)}) collective-permute-start(s32[4,4]{1,0:T(4,128)} %param.5), channel_id=1, source_target_pairs={{0,4},{4,0},{8,12},{12,8},{16,20},{20,16},{24,28},{28,24},{1,5},{5... | collective-permute-start | bytes 200 | tf_op jit(solution)/shard_map/ppermute | solution.py:17
  10.0 10.5 %collective-permute-start.6 = (bf16[64,768]{1,0:T(8,128)(2,1)}, bf16[64,768]{1,0:T(8,128)(2,1)S(1)}, u32[]{:S(2)}, u32[]{:S(2)}) collective-permute-start(bf16[64,768]{1,0:T(8,128)(2,1)} %param.4), channel_id=1, source_target_pairs={{0,16},{4,20},{8,24},{12,28},{16,0},{20,4},{24,8},{28,12},{1,17},{... | collective-permute-start | bytes 294920 | tf_op jit(solution)/shard_map/ppermute | solution.py:17
  13.0 7.8 %collective-permute-start.7 = (bf16[64,768]{1,0:T(8,128)(2,1)}, bf16[64,768]{1,0:T(8,128)(2,1)S(1)}, u32[]{:S(2)}, u32[]{:S(2)}) collective-permute-start(bf16[64,768]{1,0:T(8,128)(2,1)} %param.4), channel_id=1, source_target_pairs={{0,24},{4,28},{8,16},{12,20},{16,8},{20,12},{24,0},{28,4},{1,25},{... | collective-permute-start | bytes 294920 | tf_op jit(solution)/shard_map/ppermute | solution.py:17
  20.6 2.9 %collective-permute-start.4 = (bf16[512,768]{1,0:T(8,128)(2,1)S(1)}, bf16[512,768]{1,0:T(8,128)(2,1)S(1)}, u32[]{:S(2)}, u32[]{:S(2)}) collective-permute-start(bf16[512,768]{1,0:T(8,128)(2,1)S(1)} %bitcast.77), channel_id=1, source_target_pairs={{0,4},{4,0},{8,12},{12,8},{16,20},{20,16},{24,28},{28,24},{1,5},{5... | collective-permute-start | bytes 2359304 | tf_op jit(solution)/shard_map/ppermute | solution.py:17
  20.8 2.8 %collective-permute-start.8 = (bf16[256,768]{1,0:T(8,128)(2,1)S(1)}, bf16[256,768]{1,0:T(8,128)(2,1)S(1)}, u32[]{:S(2)}, u32[]{:S(2)}) collective-permute-start(bf16[256,768]{1,0:T(8,128)(2,1)S(1)} %bitcast.81), channel_id=1, source_target_pairs={{0,4},{4,0},{8,12},{12,8},{16,20},{20,16},{24,28},{28,24},{1,5},{5... | collective-permute-start | bytes 1179656 | tf_op jit(solution)/shard_map/ppermute | solution.py:17
  25.5 2.0 %collective-permute-start.10 = (f32[1024]{0:T(1024)S(1)}, f32[1024]{0:T(1024)S(1)}, u32[]{:S(2)}, u32[]{:S(2)}) collective-permute-start(f32[1024]{0:T(1024)S(1)} %log_add_fusion.2), channel_id=1, source_target_pairs={{0,0},{1,1},{2,2},{3,3},{4,6},{5,7},{6,4},{7,5},{8,8},{9,9},{10,10... | collective-permute-start | bytes 12296 | tf_op jit(solution)/shard_map/ppermute | solution.py:21
  26.2 1.4 %collective-permute-start.11 = (f32[1024]{0:T(1024)S(1)}, f32[1024]{0:T(1024)S(1)}, u32[]{:S(2)}, u32[]{:S(2)}) collective-permute-start(f32[1024]{0:T(1024)S(1)} %log_add_fusion.2), channel_id=1, source_target_pairs={{0,0},{1,1},{2,2},{3,3},{4,7},{5,6},{6,5},{7,4},{8,8},{9,9},{10,10... | collective-permute-start | bytes 12296 | tf_op jit(solution)/shard_map/ppermute | solution.py:21
  26.9 0.7 collective-permute-start.9
  28.3 2.0 %collective-permute-start.12 = (f32[512]{0:T(512)S(1)}, f32[512]{0:T(512)S(1)}, u32[]{:S(2)}, u32[]{:S(2)}) collective-permute-start(f32[512]{0:T(512)S(1)} %log_add_fusion.5), channel_id=1, source_target_pairs={{0,0},{1,1},{2,2},{3,3},{4,12},{5,13},{6,14},{7,15},{8,8},{9,9},{1... | collective-permute-start | bytes 6152 | tf_op jit(solution)/shard_map/ppermute | solution.py:21
  29.0 1.4 %collective-permute-start.13 = (f32[512]{0:T(512)S(1)}, f32[512]{0:T(512)S(1)}, u32[]{:S(2)}, u32[]{:S(2)}) collective-permute-start(f32[512]{0:T(512)S(1)} %log_add_fusion.5), channel_id=1, source_target_pairs={{0,0},{1,1},{2,2},{3,3},{4,20},{5,21},{6,22},{7,23},{8,8},{9,9},{1... | collective-permute-start | bytes 6152 | tf_op jit(solution)/shard_map/ppermute | solution.py:21
  29.6 0.7 collective-permute-start.14
  31.2 2.0 %collective-permute-start.15 = (f32[1024]{0:T(1024)S(1)}, f32[1024]{0:T(1024)S(1)}, u32[]{:S(2)}, u32[]{:S(2)}) collective-permute-start(f32[1024]{0:T(1024)S(1)} %log_add_fusion.1), channel_id=1, source_target_pairs={{0,0},{1,1},{2,2},{3,3},{4,5},{5,4},{6,7},{7,6},{8,8},{9,9},{10,10... | collective-permute-start | bytes 12296 | tf_op jit(solution)/shard_map/ppermute | solution.py:21
  31.8 1.4 %collective-permute-start.16 = (f32[1024]{0:T(1024)S(1)}, f32[1024]{0:T(1024)S(1)}, u32[]{:S(2)}, u32[]{:S(2)}) collective-permute-start(f32[1024]{0:T(1024)S(1)} %log_add_fusion.1), channel_id=1, source_target_pairs={{0,0},{1,1},{2,2},{3,3},{4,6},{5,7},{6,4},{7,5},{8,8},{9,9},{10,10... | collective-permute-start | bytes 12296 | tf_op jit(solution)/shard_map/ppermute | solution.py:21
  32.5 0.7 collective-permute-start.17
  33.9 2.0 %collective-permute-start.18 = (f32[512]{0:T(512)S(1)}, f32[512]{0:T(512)S(1)}, u32[]{:S(2)}, u32[]{:S(2)}) collective-permute-start(f32[512]{0:T(512)S(1)} %log_add_fusion.4), channel_id=1, source_target_pairs={{0,0},{1,1},{2,2},{3,3},{4,12},{5,13},{6,14},{7,15},{8,8},{9,9},{1... | collective-permute-start | bytes 6152 | tf_op jit(solution)/shard_map/ppermute | solution.py:21
  34.6 1.4 %collective-permute-start.19 = (f32[512]{0:T(512)S(1)}, f32[512]{0:T(512)S(1)}, u32[]{:S(2)}, u32[]{:S(2)}) collective-permute-start(f32[512]{0:T(512)S(1)} %log_add_fusion.4), channel_id=1, source_target_pairs={{0,0},{1,1},{2,2},{3,3},{4,20},{5,21},{6,22},{7,23},{8,8},{9,9},{1... | collective-permute-start | bytes 6152 | tf_op jit(solution)/shard_map/ppermute | solution.py:21
  35.2 0.7 collective-permute-start.20
  36.8 2.0 %collective-permute-start.21 = (f32[1024]{0:T(1024)S(1)}, f32[1024]{0:T(1024)S(1)}, u32[]{:S(2)}, u32[]{:S(2)}) collective-permute-start(f32[1024]{0:T(1024)S(1)} %log_add_fusion), channel_id=1, source_target_pairs={{0,0},{1,1},{2,2},{3,3},{4,5},{5,4},{6,7},{7,6},{8,8},{9,9},{10,10... | collective-permute-start | bytes 12296 | tf_op jit(solution)/shard_map/ppermute | solution.py:21
  37.4 1.4 %collective-permute-start.22 = (f32[1024]{0:T(1024)S(1)}, f32[1024]{0:T(1024)S(1)}, u32[]{:S(2)}, u32[]{:S(2)}) collective-permute-start(f32[1024]{0:T(1024)S(1)} %log_add_fusion), channel_id=1, source_target_pairs={{0,0},{1,1},{2,2},{3,3},{4,6},{5,7},{6,4},{7,5},{8,8},{9,9},{10,10... | collective-permute-start | bytes 12296 | tf_op jit(solution)/shard_map/ppermute | solution.py:21
  38.1 0.7 collective-permute-start.23
  38.8 46.4 %collective-permute-start.24 = (f32[1024]{0:T(1024)S(1)}, f32[1024]{0:T(1024)S(1)}, u32[]{:S(2)}, u32[]{:S(2)}) collective-permute-start(f32[1024]{0:T(1024)S(1)} %add_negate_fusion), channel_id=1, source_target_pairs={{0,4},{4,0},{8,12},{12,8},{16,20},{20,16},{24,28},{28,24},{1,5},{5... | collective-permute-start | bytes 12296 | tf_op jit(solution)/shard_map/ppermute | solution.py:17
  86.0 2.8 %collective-permute-start.25 = (f32[512]{0:T(512)S(1)}, f32[512]{0:T(512)S(1)}, u32[]{:S(2)}, u32[]{:S(2)}) collective-permute-start(f32[512]{0:T(512)S(1)} %log_add_fusion.3), channel_id=1, source_target_pairs={{0,0},{1,1},{2,2},{3,3},{4,12},{5,13},{6,14},{7,15},{8,8},{9,9},{1... | collective-permute-start | bytes 6152 | tf_op jit(solution)/shard_map/ppermute | solution.py:21
  86.6 2.1 %collective-permute-start.26 = (f32[512]{0:T(512)S(1)}, f32[512]{0:T(512)S(1)}, u32[]{:S(2)}, u32[]{:S(2)}) collective-permute-start(f32[512]{0:T(512)S(1)} %log_add_fusion.3), channel_id=1, source_target_pairs={{0,0},{1,1},{2,2},{3,3},{4,20},{5,21},{6,22},{7,23},{8,8},{9,9},{1... | collective-permute-start | bytes 6152 | tf_op jit(solution)/shard_map/ppermute | solution.py:21
  87.3 1.4 %collective-permute-start.27 = (f32[512]{0:T(512)S(1)}, f32[512]{0:T(512)S(1)}, u32[]{:S(2)}, u32[]{:S(2)}) collective-permute-start(f32[512]{0:T(512)S(1)} %log_add_fusion.3), channel_id=1, source_target_pairs={{0,0},{1,1},{2,2},{3,3},{4,28},{5,29},{6,30},{7,31},{8,8},{9,9},{1... | collective-permute-start | bytes 6152 | tf_op jit(solution)/shard_map/ppermute | solution.py:21
  88.8 15.5 %collective-permute-start.28 = (f32[1536]{0:T(1024)S(1)}, f32[1536]{0:T(1024)S(1)}, u32[]{:S(2)}, u32[]{:S(2)}) collective-permute-start(f32[1536]{0:T(1024)S(1)} %get-tuple-element.16), channel_id=1, source_target_pairs={{0,4},{4,0},{8,12},{12,8},{16,20},{20,16},{24,28},{28,24},{1,5},{5... | collective-permute-start | bytes 18440 | tf_op jit(solution)/shard_map/ppermute | solution.py:17
  99.2 6.0 %collective-permute-start.29 = (bf16[1,64,768]{2,1,0:T(8,128)(2,1)S(1)}, bf16[1,64,768]{2,1,0:T(8,128)(2,1)S(1)}, u32[]{:S(2)}, u32[]{:S(2)}) collective-permute-start(bf16[1,64,768]{2,1,0:T(8,128)(2,1)S(1)} %get-tuple-element.9), channel_id=1, source_target_pairs={{0,8},{4,12},{8,0},{12,4},{16,24},{20,28},{24,16},{28,20},{1,9},{5... | collective-permute-start | bytes 294920 | tf_op jit(solution)/shard_map/ppermute | solution.py:17
  99.3 10.9 %collective-permute-start.30 = (bf16[1,64,768]{2,1,0:T(8,128)(2,1)S(1)}, bf16[1,64,768]{2,1,0:T(8,128)(2,1)S(1)}, u32[]{:S(2)}, u32[]{:S(2)}) collective-permute-start(bf16[1,64,768]{2,1,0:T(8,128)(2,1)S(1)} %get-tuple-element.11), channel_id=1, source_target_pairs={{0,16},{4,20},{8,24},{12,28},{16,0},{20,4},{24,8},{28,12},{1,17},{... | collective-permute-start | bytes 294920 | tf_op jit(solution)/shard_map/ppermute | solution.py:17
  100.9 9.3 %collective-permute-start.31 = (bf16[1,64,768]{2,1,0:T(8,128)(2,1)S(1)}, bf16[1,64,768]{2,1,0:T(8,128)(2,1)S(1)}, u32[]{:S(2)}, u32[]{:S(2)}) collective-permute-start(bf16[1,64,768]{2,1,0:T(8,128)(2,1)S(1)} %get-tuple-element.10), channel_id=1, source_target_pairs={{0,24},{4,28},{8,16},{12,20},{16,8},{20,12},{24,0},{28,4},{1,25},{... | collective-permute-start | bytes 294920 | tf_op jit(solution)/shard_map/ppermute | solution.py:17
  (2 other events, 3.7 us)
where the time goes:
time: 112 us; the launch traced here: 111 us
  starting transfers between devices  83.3 us (74%)
  waiting for transfers between devices  12.9 us (12%)
  other arithmetic  6.62 us (6%)
  local copies, waits for them, and re-layouts  5.11 us (5%)
  matrix products  1.76 us (2%)
  between operations  1.3 us (1%)
    ppermute x14, starting transfers between devices, swap(): lax.ppermute(x, axis, [(i, i ^ k) for i in range(lax.axis_size(axis))])  71.4 us
    ppermute x14, waiting for transfers between devices, swap(): lax.ppermute(x, axis, [(i, i ^ k) for i in range(lax.axis_size(axis))])  12.9 us
    ppermute x18, starting transfers between devices, swap(): return lax.ppermute(x, ('row', 'col'), pairs)  11.9 us
  transfers between devices with their start and end apart: 32, of which 4 were waited for; matrix products, arithmetic and copies ran while one was open for 6% of the time, Pallas kernels for 0%

commit v1 on v0

--- a/solution.py
+++ b/solution.py
@@ -12,13 +12,8 @@
 floor_value = -1e30
 
 
-def swap(x, axis, k, one_core=False):
-    if not one_core:
-        return lax.ppermute(x, axis, [(i, i ^ k) for i in range(lax.axis_size(axis))])
-    cols = lax.axis_size("col")
-    k = k * cols if axis == "row" else k
-    pairs = [(i, i ^ k if i // cols & 1 else i) for i in range(lax.axis_size("row") * cols)]
-    return lax.ppermute(x, ("row", "col"), pairs)
+def swap(x, axis, k):
+    return lax.ppermute(x, axis, [(i, i ^ k) for i in range(lax.axis_size(axis))])
 
 
 def stages(axis):
@@ -58,7 +53,7 @@
 def log_sum_over(x, axis):
     terms = []
     for at, size in stages(axis):
-        parts = [x] + [swap(x, axis, d << at, one_core=True) for d in range(1, size)]
+        parts = [x] + [swap(x, axis, d << at) for d in range(1, size)]
         high = tree(jnp.maximum, parts)
         x = high + jnp.log(tree(jnp.add, [jnp.exp(part - high) for part in parts]))
         terms.append(parts)
@@ -92,22 +87,40 @@
     scores = jnp.where(allowed_cells, scores, floor_value)
     mass_ratio = group_cols * cols / (row_count * rows)
     log_target = -math.log(mass_ratio)
-    col_pot = jnp.zeros((group_cols,), jnp.float32)
-    for sweep in range(ITERS):
+
+    def row_pass(col_pot):
         shifted = scores + col_pot[None, :]
         row_high = jnp.max(shifted, axis=1)
         row_sum = jnp.sum(jnp.exp(shifted - row_high[:, None]), axis=1)
-        row_log, unused = log_sum_over(row_high + jnp.log(row_sum), "col")
-        row_pot = -row_log
-        if sweep == ITERS - 1:
-            row_pot = jnp.where(core == 1, row_pot, swap(row_pot, "row", 1))
+        return -log_sum_over(row_high + jnp.log(row_sum), "col")[0]
+
+    def col_pass(row_pot):
         shifted = scores + row_pot[:, None]
         col_high = jnp.max(shifted, axis=0)
         weights = jnp.exp(shifted - col_high[None, :])
         col_sum = jnp.sum(weights, axis=0)
-        col_log, terms = log_sum_over(col_high + jnp.log(col_sum), "row")
-        col_pot = log_target - col_log
+        return weights, col_sum, col_high + jnp.log(col_sum)
 
+    def rounds():
+        col_pot = jnp.zeros((group_cols,), jnp.float32)
+        for sweep in range(ITERS):
+            row_pot = row_pass(col_pot)
+            if sweep < ITERS - 1:
+                col_pot = log_target - log_sum_over(col_pass(row_pot)[2], "row")[0]
+        return row_pot
+
+    def last_logs():
+        col_log, terms = log_sum_over(part_log, "row")
+        return log_target - col_log, [part for parts in terms for part in parts]
+
+    row_pot = lax.cond(core == 1, rounds, lambda: jnp.zeros((2 * row_count,), jnp.float32))
+    row_pot = jnp.where(core == 1, row_pot, swap(row_pot, "row", 1))
+    weights, col_sum, part_log = col_pass(row_pot)
+    col_pot, flat = lax.cond(
+        core == 1,
+        last_logs,
+        lambda: (part_log, [part_log for at, size in stages("row") for d in range(size)]),
+    )
     own_weights = lax.dynamic_slice_in_dim(weights, core * half_cols, half_cols, 1)
     own_sum = lax.dynamic_slice_in_dim(col_sum, core * half_cols, half_cols, 0)
     averages = (
@@ -119,7 +132,6 @@
         )
         / own_sum[:, None]
     )
-    flat = [part for parts in terms for part in parts]
     got = swap(jnp.concatenate([col_pot] + [part[:half_cols] for part in flat]), "row", 1)
     mine = jnp.concatenate([col_pot] + [part[half_cols:] for part in flat])
     both = jnp.where(core == 1, mine, got)

time: 112 us -> 81.6 us (0.73)
  starting transfers between devices: 83.3 us -> 52.4 us
  local copies, waits for them, and re-layouts: 5.11 us -> 9.17 us
  other arithmetic: 6.62 us -> 2.9 us
  matrix products: 1.76 us -> 3.03 us
    ppermute x14, starting transfers between devices: 71.4 us -> 52.4 us  [swap(): lax.ppermute(x, axis, [(i, i ^ k) for i in range(lax.axis_size(axis))])]
    ppermute x18 -> x0, starting transfers between devices: 11.9 us -> none  [swap(): return lax.ppermute(x, ('row', 'col'), pairs)]
    reduce_sum x6 -> x1, other arithmetic: 3.14 us -> 0.46 us  [col_pass(): col_sum = jnp.sum(weights, axis=0)]
    cond x0 -> x4, local copies, waits for them, and re-layouts: none -> 1.72 us
    unnamed x10 -> x8, local copies, waits for them, and re-layouts: 0.11 us -> 1.72 us
    dot_general x1, matrix products: 0.61 us -> 2.02 us  [per_device(): lax.dot_general(own_weights.astype(jnp.bfloat16), tile_spans, (((0,), (0,...]
  transfers between devices with their start and end apart: 32 -> 14, of which waited for: 4 -> 5; matrix products, arithmetic and copies ran while one was open for 6% -> 10% of each run, Pallas kernels for 0% -> 0%
where the time goes in v1:
time: 81.6 us; the launch traced here: 81.3 us
  starting transfers between devices  52.4 us (64%)
  waiting for transfers between devices  12.9 us (16%)
  local copies, waits for them, and re-layouts  9.17 us (11%)
  matrix products  3.03 us (4%)
  other arithmetic  2.9 us (4%)
  between operations  0.9 us (1%)
    ppermute x14, starting transfers between devices, swap(): lax.ppermute(x, axis, [(i, i ^ k) for i in range(lax.axis_size(axis))])  52.4 us
    ppermute x14, waiting for transfers between devices, swap(): lax.ppermute(x, axis, [(i, i ^ k) for i in range(lax.axis_size(axis))])  12.9 us
    dynamic_update_slice x14, local copies, waits for them, and re-layouts, place(): whole = lax.dynamic_update_index_in_dim(whole, part, index ^ d, 0)  2.21 us
    dot_general x1, matrix products, per_device(): lax.dot_general(own_weights.astype(jnp.bfloat16), tile_spans, (((0,), (0,...  2.02 us
    cond x4, local copies, waits for them, and re-layouts  1.72 us
    unnamed x8, local copies, waits for them, and re-layouts  1.72 us
  transfers between devices with their start and end apart: 14, of which 5 were waited for; matrix products, arithmetic and copies ran while one was open for 10% of the time, Pallas kernels for 0%

profile of v1, /device:TPU:0, one launch (start us, length us, event | category | flops | bytes accessed | tf_op | source)
XLA Modules:
  0.0 81.3 jit_solution(12892776369223668064)
XLA Ops:
  0.6 3.0 %collective-permute-start.19 = (bf16[128,768]{1,0:T(8,128)(2,1)}, bf16[128,768]{1,0:T(8,128)(2,1)S(1)}, u32[]{:S(2)}, u32[]{:S(2)}) collective-permute-start(bf16[128,768]{1,0:T(8,128)(2,1)} %param.7), channel_id=1, source_target_pairs={{0,1},{1,0},{2,3},{3,2},{4,5},{5,4},{6,7},{7,6},{8,9},{9,8},{10,11... | collective-permute-start | bytes 589832 | tf_op jit(solution)/shard_map/ppermute | solution.py:16
  3.6 1.5 %collective-permute-start.20 = (bf16[128,768]{1,0:T(8,128)(2,1)}, bf16[128,768]{1,0:T(8,128)(2,1)S(1)}, u32[]{:S(2)}, u32[]{:S(2)}) collective-permute-start(bf16[128,768]{1,0:T(8,128)(2,1)} %param.7), channel_id=1, source_target_pairs={{0,2},{1,3},{2,0},{3,1},{4,6},{5,7},{6,4},{7,5},{8,10},{9,11},{10,... | collective-permute-start | bytes 589832 | tf_op jit(solution)/shard_map/ppermute | solution.py:16
  5.2 2.0 %collective-permute-start.23 = (bf16[64,768]{1,0:T(8,128)(2,1)}, bf16[64,768]{1,0:T(8,128)(2,1)S(1)}, u32[]{:S(2)}, u32[]{:S(2)}) collective-permute-start(bf16[64,768]{1,0:T(8,128)(2,1)} %param.8), channel_id=1, source_target_pairs={{0,8},{4,12},{8,0},{12,4},{16,24},{20,28},{24,16},{28,20},{1,9},{5... | collective-permute-start | bytes 294920 | tf_op jit(solution)/shard_map/ppermute | solution.py:16
  7.2 0.8 copy.16
  8.1 0.9 %bitcast_dynamic-update-slice_fusion.7 = bf16[4,128,768]{2,1,0:T(8,128)(2,1)S(1)} fusion(bf16[4,128,768]{2,1,0:T(8,128)(2,1)S(1)} %broadcast_in_dim.89, s32[]{:T(128)S(6)} %select_n.138, bf16[128,768]{1,0:T(8,128)(2,1)} %param.7), kind=kLoop, calls=%fused_computation.67 | loop fusion | bytes 393220 | tf_op jit(solution)/shard_map/jit(dynamic_update_index_in_dim)/dynamic_update_slice | solution.py:32
  9.1 0.9 %bitcast_dynamic-update-slice_fusion.11 = bf16[4,64,768]{2,1,0:T(8,128)(2,1)S(1)} fusion(bf16[4,64,768]{2,1,0:T(8,128)(2,1)S(1)} %broadcast_in_dim.97, s32[]{:T(128)S(6)} %select_n.142, bf16[64,768]{1,0:T(8,128)(2,1)} %param.8), kind=kLoop, calls=%fused_computation.72 | loop fusion | bytes 196612 | tf_op jit(solution)/shard_map/jit(dynamic_update_index_in_dim)/dynamic_update_slice | solution.py:32
  10.0 2.7 %collective-permute-start.24 = (bf16[64,768]{1,0:T(8,128)(2,1)}, bf16[64,768]{1,0:T(8,128)(2,1)S(1)}, u32[]{:S(2)}, u32[]{:S(2)}) collective-permute-start(bf16[64,768]{1,0:T(8,128)(2,1)} %param.8), channel_id=1, source_target_pairs={{0,16},{4,20},{8,24},{12,28},{16,0},{20,4},{24,8},{28,12},{1,17},{... | collective-permute-start | bytes 294920 | tf_op jit(solution)/shard_map/ppermute | solution.py:16
  13.0 1.1 %collective-permute-start.25 = (bf16[64,768]{1,0:T(8,128)(2,1)}, bf16[64,768]{1,0:T(8,128)(2,1)S(1)}, u32[]{:S(2)}, u32[]{:S(2)}) collective-permute-start(bf16[64,768]{1,0:T(8,128)(2,1)} %param.8), channel_id=1, source_target_pairs={{0,24},{4,28},{8,16},{12,20},{16,8},{20,12},{24,0},{28,4},{1,25},{... | collective-permute-start | bytes 294920 | tf_op jit(solution)/shard_map/ppermute | solution.py:16
  14.1 6.4 %collective-permute-done.24 = bf16[64,768]{1,0:T(8,128)(2,1)S(1)} collective-permute-done((bf16[64,768]{1,0:T(8,128)(2,1)}, bf16[64,768]{1,0:T(8,128)(2,1)S(1)}, u32[]{:S(2)}, u32[]{:S(2)}) %collective-permute-start.24) | collective-permute-done | bytes 98336 | tf_op jit(solution)/shard_map/ppermute | solution.py:16
  20.8 0.5 collective-permute-start.26
  21.3 1.3 %compare_reduce_fusion = pred[1024,512]{1,0:T(8,128)(4,1)S(1)} fusion(s32[512]{0:T(512)S(1)} %add_select_fusion, s32[1024,4]{0,1:T(4,128)S(1)} %bitcast.86), kind=kLoop, calls=%fused_computation.50 | loop fusion | flops 3670016 | bytes 542720 | tf_op jit(solution)/shard_map/reduce_or | solution.py:80
  22.9 0.7 collective-permute-done.26
  23.7 1.0 %multiply_select_fusion = f32[1024,512]{1,0:T(8,128)S(1)} fusion(pred[1024,512]{1,0:T(8,128)(4,1)S(1)} %compare_reduce_fusion, bf16[1024,768]{1,0:T(8,128)(2,1)S(1)} %bitcast.79, bf16[512,768]{1,0:T(8,128)(2,1)S(1)} %bitcast.85), kind=kOutput, calls=%fused_computation.52 | convolution fusion | flops 806354944 | bytes 4980736 | tf_op jit(solution)/shard_map/dot_general | solution.py:82
  24.8 31.5 %collective-permute-start.27 = (f32[1024]{0:T(1024)S(1)}, f32[1024]{0:T(1024)S(1)}, u32[]{:S(2)}, u32[]{:S(2)}) collective-permute-start(f32[1024]{0:T(1024)S(1)} %get-tuple-element.48), channel_id=1, source_target_pairs={{0,4},{4,0},{8,12},{12,8},{16,20},{20,16},{24,28},{28,24},{1,5},{5... | collective-permute-start | bytes 12296 | tf_op jit(solution)/shard_map/ppermute | solution.py:16
  56.3 0.8 %collective-permute-done.27 = f32[1024]{0:T(1024)S(1)} collective-permute-done((f32[1024]{0:T(1024)S(1)}, f32[1024]{0:T(1024)S(1)}, u32[]{:S(2)}, u32[]{:S(2)}) %collective-permute-start.27) | collective-permute-done | bytes 4128 | tf_op jit(solution)/shard_map/ppermute | solution.py:16
  57.2 0.2 add_reduce_fusion.4
  57.4 0.5 fusion.46
  57.9 1.7 %conditional.3 = (f32[512]{0:T(512)S(1)}, f32[512]{0:T(512)}, f32[512]{0:T(512)}, f32[512]{0:T(512)}) conditional(s32[]{:T(128)} %convert_element_type.33, f32[512]{0:T(512)S(1)} %log_add_fusion.5, f32[512]{0:T(512)S(1)} %log_add_fusion.5), branch_computations={%region_15.16_spmd, %region_16.17_spmd} | conditional | flops 6144 | bytes 34968 | solution.py:119
  57.9 0.6 copy.39
  58.5 0.6 copy.40
  59.0 0.6 copy.41
  59.6 0.7 constant_dynamic-update-slice_fusion.5
  60.4 0.8 constant_dynamic-update-slice_fusion.3
  61.1 0.7 constant_dynamic-update-slice_fusion.1
  61.9 5.5 %collective-permute-start.28 = (f32[1536]{0:T(1024)S(1)}, f32[1536]{0:T(1024)S(1)}, u32[]{:S(2)}, u32[]{:S(2)}) collective-permute-start(f32[1536]{0:T(1024)S(1)} %get-tuple-element.28), channel_id=1, source_target_pairs={{0,4},{4,0},{8,12},{12,8},{16,20},{20,16},{24,28},{28,24},{1,5},{5... | collective-permute-start | bytes 18440 | tf_op jit(solution)/shard_map/ppermute | solution.py:16
  67.4 2.0 %convolution_divide_fusion = f32[256,768]{1,0:T(8,128)S(1)} fusion(bf16[1024,768]{1,0:T(8,128)(2,1)} %bitcast.80, bf16[1024,512]{1,0:T(8,128)(2,1)S(1)} %get-tuple-element.20, s32[]{:T(128)S(6)} %select_n.150, f32[256]{0:T(256)S(1)} %dynamic_slice.29), kind=kOutput, calls=%fused_computation.54 | convolution fusion | flops 402849792 | bytes 2884612 | tf_op jit(solution)/shard_map/dot_general | solution.py:127
  69.6 2.6 %collective-permute-start.30 = (bf16[1,64,768]{2,1,0:T(8,128)(2,1)S(1)}, bf16[1,64,768]{2,1,0:T(8,128)(2,1)S(1)}, u32[]{:S(2)}, u32[]{:S(2)}) collective-permute-start(bf16[1,64,768]{2,1,0:T(8,128)(2,1)S(1)} %get-tuple-element.23), channel_id=1, source_target_pairs={{0,16},{4,20},{8,24},{12,28},{16,0},{20,4},{24,8},{28,12},{1,17},{... | collective-permute-start | bytes 294920 | tf_op jit(solution)/shard_map/ppermute | solution.py:16
  72.2 1.7 %collective-permute-start.31 = (bf16[1,64,768]{2,1,0:T(8,128)(2,1)S(1)}, bf16[1,64,768]{2,1,0:T(8,128)(2,1)S(1)}, u32[]{:S(2)}, u32[]{:S(2)}) collective-permute-start(bf16[1,64,768]{2,1,0:T(8,128)(2,1)S(1)} %get-tuple-element.22), channel_id=1, source_target_pairs={{0,24},{4,28},{8,16},{12,20},{16,8},{20,12},{24,0},{28,4},{1,25},{... | collective-permute-start | bytes 294920 | tf_op jit(solution)/shard_map/ppermute | solution.py:16
  74.0 0.6 dynamic_slice.34
  74.9 0.7 reshape.273
  75.6 4.9 %collective-permute-done.30 = bf16[1,64,768]{2,1,0:T(8,128)(2,1)S(1)} collective-permute-done((bf16[1,64,768]{2,1,0:T(8,128)(2,1)S(1)}, bf16[1,64,768]{2,1,0:T(8,128)(2,1)S(1)}, u32[]{:S(2)}, u32[]{:S(2)}) %collective-permute-start.30) | collective-permute-done | bytes 98336 | tf_op jit(solution)/shard_map/ppermute | solution.py:16
  80.5 0.8 fusion.21
  (60 shorter events, 1.7 us)
Async XLA Ops:
  0.6 19.9 %collective-permute-start.19 = (bf16[128,768]{1,0:T(8,128)(2,1)}, bf16[128,768]{1,0:T(8,128)(2,1)S(1)}, u32[]{:S(2)}, u32[]{:S(2)}) collective-permute-start(bf16[128,768]{1,0:T(8,128)(2,1)} %param.7), channel_id=1, source_target_pairs={{0,1},{1,0},{2,3},{3,2},{4,5},{5,4},{6,7},{7,6},{8,9},{9,8},{10,11... | collective-permute-start | bytes 589832 | tf_op jit(solution)/shard_map/ppermute | solution.py:16
  3.6 16.9 %collective-permute-start.20 = (bf16[128,768]{1,0:T(8,128)(2,1)}, bf16[128,768]{1,0:T(8,128)(2,1)S(1)}, u32[]{:S(2)}, u32[]{:S(2)}) collective-permute-start(bf16[128,768]{1,0:T(8,128)(2,1)} %param.7), channel_id=1, source_target_pairs={{0,2},{1,3},{2,0},{3,1},{4,6},{5,7},{6,4},{7,5},{8,10},{9,11},{10,... | collective-permute-start | bytes 589832 | tf_op jit(solution)/shard_map/ppermute | solution.py:16
  5.2 15.5 %collective-permute-start.21 = (bf16[128,768]{1,0:T(8,128)(2,1)}, bf16[128,768]{1,0:T(8,128)(2,1)S(1)}, u32[]{:S(2)}, u32[]{:S(2)}) collective-permute-start(bf16[128,768]{1,0:T(8,128)(2,1)} %param.7), channel_id=1, source_target_pairs={{0,3},{1,2},{2,1},{3,0},{4,7},{5,6},{6,5},{7,4},{8,11},{9,10},{10,... | collective-permute-start | bytes 589832 | tf_op jit(solution)/shard_map/ppermute | solution.py:16
  5.2 7.8 %collective-permute-start.23 = (bf16[64,768]{1,0:T(8,128)(2,1)}, bf16[64,768]{1,0:T(8,128)(2,1)S(1)}, u32[]{:S(2)}, u32[]{:S(2)}) collective-permute-start(bf16[64,768]{1,0:T(8,128)(2,1)} %param.8), channel_id=1, source_target_pairs={{0,8},{4,12},{8,0},{12,4},{16,24},{20,28},{24,16},{28,20},{1,9},{5... | collective-permute-start | bytes 294920 | tf_op jit(solution)/shard_map/ppermute | solution.py:16
  7.2 2.8 %collective-permute-start.18 = (s32[4,4]{1,0:T(4,128)}, s32[4,4]{1,0:T(4,128)S(1)}, u32[]{:S(2)}, u32[]{:S(2)}) collective-permute-start(s32[4,4]{1,0:T(4,128)} %param.9), channel_id=1, source_target_pairs={{0,4},{4,0},{8,12},{12,8},{16,20},{20,16},{24,28},{28,24},{1,5},{5... | collective-permute-start | bytes 200 | tf_op jit(solution)/shard_map/ppermute | solution.py:16
  10.0 10.5 %collective-permute-start.24 = (bf16[64,768]{1,0:T(8,128)(2,1)}, bf16[64,768]{1,0:T(8,128)(2,1)S(1)}, u32[]{:S(2)}, u32[]{:S(2)}) collective-permute-start(bf16[64,768]{1,0:T(8,128)(2,1)} %param.8), channel_id=1, source_target_pairs={{0,16},{4,20},{8,24},{12,28},{16,0},{20,4},{24,8},{28,12},{1,17},{... | collective-permute-start | bytes 294920 | tf_op jit(solution)/shard_map/ppermute | solution.py:16
  13.0 7.8 %collective-permute-start.25 = (bf16[64,768]{1,0:T(8,128)(2,1)}, bf16[64,768]{1,0:T(8,128)(2,1)S(1)}, u32[]{:S(2)}, u32[]{:S(2)}) collective-permute-start(bf16[64,768]{1,0:T(8,128)(2,1)} %param.8), channel_id=1, source_target_pairs={{0,24},{4,28},{8,16},{12,20},{16,8},{20,12},{24,0},{28,4},{1,25},{... | collective-permute-start | bytes 294920 | tf_op jit(solution)/shard_map/ppermute | solution.py:16
  20.6 2.9 %collective-permute-start.22 = (bf16[512,768]{1,0:T(8,128)(2,1)S(1)}, bf16[512,768]{1,0:T(8,128)(2,1)S(1)}, u32[]{:S(2)}, u32[]{:S(2)}) collective-permute-start(bf16[512,768]{1,0:T(8,128)(2,1)S(1)} %bitcast.77), channel_id=1, source_target_pairs={{0,4},{4,0},{8,12},{12,8},{16,20},{20,16},{24,28},{28,24},{1,5},{5... | collective-permute-start | bytes 2359304 | tf_op jit(solution)/shard_map/ppermute | solution.py:16
  20.8 2.8 %collective-permute-start.26 = (bf16[256,768]{1,0:T(8,128)(2,1)S(1)}, bf16[256,768]{1,0:T(8,128)(2,1)S(1)}, u32[]{:S(2)}, u32[]{:S(2)}) collective-permute-start(bf16[256,768]{1,0:T(8,128)(2,1)S(1)} %bitcast.81), channel_id=1, source_target_pairs={{0,4},{4,0},{8,12},{12,8},{16,20},{20,16},{24,28},{28,24},{1,5},{5... | collective-permute-start | bytes 1179656 | tf_op jit(solution)/shard_map/ppermute | solution.py:16
  23.7 1.2 %copy-start = (bf16[2,512,768]{2,1,0:T(8,128)(2,1)}, bf16[2,512,768]{2,1,0:T(8,128)(2,1)S(1)}, u32[]{:S(2)}) copy-start(bf16[2,512,768]{2,1,0:T(8,128)(2,1)S(1)} %bitcast_dynamic-update-slice_fusion) | copy-start | bytes 4718596
  24.8 32.3 %collective-permute-start.27 = (f32[1024]{0:T(1024)S(1)}, f32[1024]{0:T(1024)S(1)}, u32[]{:S(2)}, u32[]{:S(2)}) collective-permute-start(f32[1024]{0:T(1024)S(1)} %get-tuple-element.48), channel_id=1, source_target_pairs={{0,4},{4,0},{8,12},{12,8},{16,20},{20,16},{24,28},{28,24},{1,5},{5... | collective-permute-start | bytes 12296 | tf_op jit(solution)/shard_map/ppermute | solution.py:16
  61.9 12.8 %collective-permute-start.28 = (f32[1536]{0:T(1024)S(1)}, f32[1536]{0:T(1024)S(1)}, u32[]{:S(2)}, u32[]{:S(2)}) collective-permute-start(f32[1536]{0:T(1024)S(1)} %get-tuple-element.28), channel_id=1, source_target_pairs={{0,4},{4,0},{8,12},{12,8},{16,20},{20,16},{24,28},{28,24},{1,5},{5... | collective-permute-start | bytes 18440 | tf_op jit(solution)/shard_map/ppermute | solution.py:16
  69.5 6.1 %collective-permute-start.29 = (bf16[1,64,768]{2,1,0:T(8,128)(2,1)S(1)}, bf16[1,64,768]{2,1,0:T(8,128)(2,1)S(1)}, u32[]{:S(2)}, u32[]{:S(2)}) collective-permute-start(bf16[1,64,768]{2,1,0:T(8,128)(2,1)S(1)} %get-tuple-element.21), channel_id=1, source_target_pairs={{0,8},{4,12},{8,0},{12,4},{16,24},{20,28},{24,16},{28,20},{1,9},{5... | collective-permute-start | bytes 294920 | tf_op jit(solution)/shard_map/ppermute | solution.py:16
  69.6 10.9 %collective-permute-start.30 = (bf16[1,64,768]{2,1,0:T(8,128)(2,1)S(1)}, bf16[1,64,768]{2,1,0:T(8,128)(2,1)S(1)}, u32[]{:S(2)}, u32[]{:S(2)}) collective-permute-start(bf16[1,64,768]{2,1,0:T(8,128)(2,1)S(1)} %get-tuple-element.23), channel_id=1, source_target_pairs={{0,16},{4,20},{8,24},{12,28},{16,0},{20,4},{24,8},{28,12},{1,17},{... | collective-permute-start | bytes 294920 | tf_op jit(solution)/shard_map/ppermute | solution.py:16
  72.2 8.3 %collective-permute-start.31 = (bf16[1,64,768]{2,1,0:T(8,128)(2,1)S(1)}, bf16[1,64,768]{2,1,0:T(8,128)(2,1)S(1)}, u32[]{:S(2)}, u32[]{:S(2)}) collective-permute-start(bf16[1,64,768]{2,1,0:T(8,128)(2,1)S(1)} %get-tuple-element.22), channel_id=1, source_target_pairs={{0,24},{4,28},{8,16},{12,20},{16,8},{20,12},{24,0},{28,4},{1,25},{... | collective-permute-start | bytes 294920 | tf_op jit(solution)/shard_map/ppermute | solution.py:16
